TPU v7x, 128 devices: a whole 4x4x4 slice. The times are simulated.
128 devices in a mesh: run: 4 (over y), prec: 32 (over x, z, core).
Axes of the slice: x: 4, y: 4, z: 4, core: 2. Of those that a mesh axis runs over, the one named last changes fastest.
Arguments:
- chromatograms: bfloat16 [32, 65536, 256], P('run', 'prec'), may hold values from 0.049804688 to 20
- standards: int32 [32, 11], P('run'), may hold values from 0 to 255, as said below
- library: int32 [11], replicated, may hold values from 0 to 255, as said below
- owner_of: int32 [65536, 1], P('prec'), may hold values from 0 to 31; in each aligned block of 512 rows (0 to 511, 512 to 1023, ...) at most 32 rows name the same one
- local_group: int32 [65536], P('prec'), may hold values from 0 to 511
- quality: bfloat16 [65536], P('prec'), may hold values from 0.25 to 4
Outputs:
- summary: bfloat16 [32, 16384, 256], P('run', 'prec')
Inputs may be any that keep to these rules, and one draw needn't show every extreme that they name: library starts at 0, ends at 255 and rises strictly. `standards`: each run's row starts at 0, ends at 255 and rises strictly. `owner_of`: in each aligned block of 512 rows no owner is named more than 32 times.
All inputs are finite; a program needn't handle non-finite values.
Results may differ from a plain program's by a relative error of at most 0.004.
Values may be sent and summed in bfloat16 or wider, within the bound.
A program may use at most 128 MiB of HBM per device.

v0:
```python
import jax
import jax.numpy as jnp
from jax import lax
from jax.sharding import PartitionSpec as P

GRP_DEV = 512


def warp_matrices(standards, library, width):
    count = library.shape[0]
    points = jnp.arange(width, dtype=jnp.int32)
    t_float = points.astype(jnp.float32)
    segment = jnp.sum(
        (library[1 : count - 1][None, :] <= points[:, None]).astype(jnp.int32), axis=1
    )
    pick = (segment[:, None] == jnp.arange(count - 1, dtype=jnp.int32)[None, :]).astype(jnp.float32)
    lib_f = library.astype(jnp.float32)
    obs_f = standards.astype(jnp.float32)
    slope = (obs_f[:, 1:] - obs_f[:, :-1]) / (lib_f[1:] - lib_f[:-1])[None, :]
    mapped = (
        obs_f[:, None, :-1] + (t_float[None, :, None] - lib_f[None, None, :-1]) * slope[:, None, :]
    )
    source = jnp.sum(mapped * pick[None], axis=2)
    tent = jnp.maximum(0.0, 1.0 - jnp.abs(source[:, :, None] - t_float[None, None, :]))
    return tent.astype(jnp.bfloat16)


def slot_places(target, owners, capacity):
    hit = (target[:, None] == jnp.arange(owners, dtype=jnp.int32)[None, :]).astype(jnp.int32)
    before = jnp.cumsum(hit, axis=0) - hit
    return target * capacity + jnp.sum(before * hit, axis=1)


def slot_sources(place, slots):
    rows = jnp.arange(place.shape[0], dtype=jnp.int32)
    return jnp.zeros((slots,), jnp.int32).at[place].set(rows)


def fill_slots(values, source_row):
    return jnp.take(values, source_row, axis=1)


def align_rows(tent, values, weight):
    resampled = jnp.einsum("rpj,rtj->rpt", values, tent, preferred_element_type=jnp.float32)
    return (weight[:, :, None] * jnp.log1p(resampled)).astype(jnp.bfloat16)


def membership(tags):
    return (jnp.arange(GRP_DEV, dtype=jnp.int32)[:, None] == tags[None, :]).astype(jnp.bfloat16)


def per_device(chromatograms, standards, library, owner_of, local_group, quality):
    owners = lax.axis_size("prec")
    run_count = lax.axis_size("run")
    run_dev, p_dev, width = chromatograms.shape
    p_sub = p_dev // run_count
    most = max(2, 2 * p_sub // owners)
    capacity = run_count * most
    slots = owners * capacity
    tent = warp_matrices(standards, library, width)
    place = slot_places(owner_of[:, 0], owners, capacity)
    source_row = slot_sources(place, slots)
    tags = jnp.full((slots,), -1, jnp.int32).at[place].set(local_group)
    got_tags = lax.all_to_all(tags, "prec", split_axis=0, concat_axis=0, tiled=True)
    member = membership(got_tags)
    profile = align_rows(tent, chromatograms, quality.astype(jnp.float32)[None, :])
    buffer = fill_slots(profile, source_row)
    received = lax.all_to_all(buffer, "prec", split_axis=1, concat_axis=1, tiled=True)
    member_runs = jnp.broadcast_to(member[None], (received.shape[0],) + member.shape)
    totals = jnp.einsum("ags,asp->agp", member_runs, received, preferred_element_type=jnp.float32)
    return (0.25 * totals).astype(jnp.bfloat16)


def solution(mesh):
    placed = (P("run", "prec", None), P("run", None), P(), P("prec", None), P("prec"), P("prec"))
    return jax.shard_map(
        per_device, mesh=mesh, in_specs=placed, out_specs=P("run", "prec", None), check_vma=False
    )
```

profile of v0, /device:TPU:52, one launch (start us, length us, event | category | flops | bytes accessed | tf_op | source)
XLA Modules:
  0.0 408.7 jit_solution(6362717998114565386)
XLA Ops:
  0.0 0.7 fusion.16
  0.7 9.1 %reduce-window.6 = s32[32,16,128]{2,1,0:T(8,128)S(1)} reduce-window(s32[32,16,128]{2,1,0:T(8,128)S(1)} %fusion.16, s32[]{:T(128)} %constant.12.clone.1), window={size=1x1x128 pad=0_0x0_0x127_0}, to_apply=%region_0.0 | reduce-window | flops 8323072 | bytes 524292 | tf_op jit(solution)/shard_map/reduce-window
  9.8 0.1 slice.32
  9.9 0.2 copy.22
  10.2 0.2 reduce-window.9
  10.4 0.1 broadcast_add_fusion
  10.5 0.8 fusion.15
  11.3 0.7 compare_select_fusion
  12.1 8.8 %scatter_custom_fusion = s32[4096]{0:T(1024)} fusion(s32[2048]{0:T(1024)S(1)} %bitcast.40, s32[2048]{0:T(1024)} %param.10, s32[]{:T(128)} %constant.10.clone.1), kind=kCustom, calls=%fused_computation.37 | custom fusion | bytes 16896 | tf_op jit(solution)/shard_map/scatter | solution.py:63
  20.8 8.0 %all-to-all-start = ((s32[32,128,1]{1,2,0:T(1,128)}), s32[32,128,1]{1,2,0:T(1,128)S(1)}, u32[]{:S(2)}, u32[]{:S(2)}) async-start(s32[32,128,1]{1,2,0:T(1,128)} %bitcast.8), calls=%async_computation | async-start | bytes 32768 | tf_op jit(solution)/shard_map/all_to_all | solution.py:64
  28.9 0.7 convert_element_type.64
  29.5 0.7 slice.29
  30.2 8.1 %scatter_custom_fusion.1 = s32[4096]{0:T(1024)S(1)} fusion(s32[2048]{0:T(1024)S(1)} %bitcast.41, s32[2048]{0:T(1024)S(1)} %iota.38, s32[]{:T(128)} %constant.12.clone.1), kind=kCustom, calls=%fused_computation.35 | custom fusion | bytes 16388 | tf_op jit(solution)/shard_map/scatter | solution.py:36
  38.4 0.7 convert_element_type.62
  39.3 0.1 convert_reduce_fusion
  39.4 0.7 convert_element_type.61
  40.3 12.7 %fusion.3 = bf16[8,2048,256]{1,2,0:T(8,128)(2,1)} fusion(f32[2048]{0:T(1024)S(1)} %convert_element_type.61, bf16[8,2048,256]{2,1,0:T(8,128)(2,1)} %param.6, f32[256]{0:T(256)S(1)} %iota_convert_fusion, f32[8,256]{1,0:T(8,128)S(1)} %multiply_reduce_fusion), kind=kOutput, calls=%fused_computation.8 | convolution fusion | flops 2158493696 | bytes 16794624 | tf_op jit(solution)/shard_map/rpj,rtj->rpt/dot_general | solution.py:44
  53.0 12.6 %copy.20 = bf16[8,2048,256]{2,0,1:T(8,128)(2,1)} copy(bf16[8,2048,256]{1,2,0:T(8,128)(2,1)} %fusion.3) | data formatting | bytes 16777216 | tf_op jit(solution)/shard_map/convert_element_type | solution.py:45
  65.6 34.6 %gather_fusion = bf16[4096,8,256]{2,1,0:T(8,128)(2,1)} fusion(bf16[8,2048,256]{2,0,1:T(8,128)(2,1)} %copy.20, s32[4096]{0:T(1024)S(1)} %fusion.18), kind=kCustom, calls=%fused_computation | custom fusion | bytes 33570816 | tf_op jit(solution)/shard_map/jit(_take)/gather | solution.py:40
  100.2 16.8 %select_bitcast_fusion = bf16[8,4096,256]{2,0,1:T(8,128)(2,1)} fusion(bf16[4096,8,256]{2,1,0:T(8,128)(2,1)} %gather_fusion, pred[4096]{0:T(1024)(128)(4,1)S(1)} %compare_and_fusion), kind=kLoop, calls=%fused_computation.3 | loop fusion | flops 8388608 | bytes 33558528 | tf_op jit(solution)/shard_map/jit(_take)/select_n | solution.py:40
  117.0 7.5 %all-to-all-start.1 = ((bf16[8,4096,256]{2,0,1:T(8,128)(2,1)}), bf16[8,4096,256]{2,0,1:T(8,128)(2,1)}, u32[]{:S(2)}, u32[]{:S(2)}) async-start(bf16[8,4096,256]{2,0,1:T(8,128)(2,1)} %select_bitcast_fusion), calls=%async_computation.1 | async-start | bytes 33554432 | tf_op jit(solution)/shard_map/all_to_all | solution.py:68
  124.5 3.2 fusion.4
  127.7 266.3 %all-to-all-done.1 = bf16[8,4096,256]{2,0,1:T(8,128)(2,1)} async-done(((bf16[8,4096,256]{2,0,1:T(8,128)(2,1)}), bf16[8,4096,256]{2,0,1:T(8,128)(2,1)}, u32[]{:S(2)}, u32[]{:S(2)}) %all-to-all-start.1) | async-done | bytes 16777248 | tf_op jit(solution)/shard_map/all_to_all | solution.py:68
  393.9 14.7 %multiply_convert_fusion.1 = bf16[8,512,256]{2,1,0:T(8,128)(2,1)} fusion(bf16[8,4096,256]{2,0,1:T(8,128)(2,1)} %all-to-all-done.1, bf16[512,4096]{1,0:T(8,128)(2,1)} %fusion.4), kind=kOutput, calls=%fused_computation.11 | convolution fusion | flops 8592031744 | bytes 23068672 | tf_op jit(solution)/shard_map/ags,asp->agp/dot_general | solution.py:70
  (12 shorter events, 0.5 us)
Async XLA Ops:
  20.8 96.1 %all-to-all-start = ((s32[32,128,1]{1,2,0:T(1,128)}), s32[32,128,1]{1,2,0:T(1,128)S(1)}, u32[]{:S(2)}, u32[]{:S(2)}) async-start(s32[32,128,1]{1,2,0:T(1,128)} %bitcast.8), calls=%async_computation | async-start | bytes 32768 | tf_op jit(solution)/shard_map/all_to_all | solution.py:64
  117.0 277.0 %all-to-all-start.1 = ((bf16[8,4096,256]{2,0,1:T(8,128)(2,1)}), bf16[8,4096,256]{2,0,1:T(8,128)(2,1)}, u32[]{:S(2)}, u32[]{:S(2)}) async-start(bf16[8,4096,256]{2,0,1:T(8,128)(2,1)} %select_bitcast_fusion), calls=%async_computation.1 | async-start | bytes 33554432 | tf_op jit(solution)/shard_map/all_to_all | solution.py:68
where the time goes:
time: 409 us
  waiting for transfers between devices  266 us (65%)
  local copies, waits for them, and re-layouts  65.2 us (16%)
  other arithmetic  34.2 us (8%)
  matrix products  27.5 us (7%)
  starting transfers between devices  15.5 us (4%)
    all_to_all x1, waiting for transfers between devices, per_device(): lax.all_to_all(buffer, 'prec', split_axis=1, concat_axis=1, tiled=True)  266 us
    gather x1, local copies, waits for them, and re-layouts, fill_slots(): return jnp.take(values, source_row, axis=1)  34.6 us
    select_n x1, other arithmetic, fill_slots(): return jnp.take(values, source_row, axis=1)  16.8 us
    dot_general x1, matrix products, per_device(): jnp.einsum('ags,asp->agp', member_runs, received, preferred_element_type=...  14.7 us
    dot_general x1, matrix products, align_rows(): jnp.einsum('rpj,rtj->rpt', values, tent, preferred_element_type=jnp.float32)  12.7 us
    convert_element_type x1, local copies, waits for them, and re-layouts, align_rows(): return (weight[:, :, None] * jnp.log1p(resampled)).astype(jnp.bfloat16)  12.6 us
    another operation x3, other arithmetic  9.41 us
    scatter x1, local copies, waits for them, and re-layouts, per_device(): tags = jnp.full((slots,), -1, jnp.int32).at[place].set(local_group)  8.79 us
  transfers between devices with their start and end apart: 2, of which 1 were waited for; matrix products, arithmetic and copies ran while one was open for 22% of the time, Pallas kernels for 0%

commit v1 on v0

v1 whole, which is shorter than its diff:
```python
import jax
import jax.numpy as jnp
from jax import lax
from jax.experimental import pallas as pl
from jax.experimental.pallas import tpu as pltpu
from jax.sharding import PartitionSpec as P

MESH = pl.DeviceIdType.MESH
F32 = jnp.float32
BF16 = jnp.bfloat16
RUNS = 8
BLOCKS = 4
BLOCK = 512
MOST = 32
OWNERS = 32
GRP = 512
PTS = 256
STANDARDS = 11
SIDE = 4
LINE = 8
SLOTS = 4


def nt_dot(a, b):
    return lax.dot_general(a, b, (((1,), (1,)), ((), ())), preferred_element_type=F32)


def kernel(
    x_hbm, std, lib, own, lg, q, out,
    xbuf, perm, tri, qcol, srcs, tags, rtags, member, sbuf, rbuf, dbuf, ddbuf, mine,
    x_sem, tag_ssem, tag_rsem, s_sem, r_sem, d_sem, dd_sem,
):
    yy = lax.axis_index("run")
    pp = lax.axis_index("prec")
    xx, zz, cc = pp // 8, (pp // 2) % 4, pp % 2

    def along(order, first, second, core):
        gx = (1 - order) * first + order * second
        gz = (1 - order) * second + order * first
        return gx * 8 + gz * 2 + core

    def load(j):
        return pltpu.make_async_copy(x_hbm.at[j], xbuf.at[j % 2], x_sem.at[j % 2])

    barrier = pltpu.get_barrier_semaphore()
    for order in range(2):
        first = (xx, zz)[order]
        second = (zz, xx)[order]
        for df in range(SIDE):
            for dc in range(2):
                if (df, dc) == (0, 0) or (order == 1 and df == 0):
                    continue
                other = along(order, (first + df) % SIDE, second, (cc + dc) % 2)
                pl.semaphore_signal(barrier, inc=1, device_id=(yy, other), device_id_type=MESH)
    load(0).start()
    load(1).start()

    t = lax.broadcasted_iota(jnp.int32, (1, PTS), 1)
    later = [lib[k] <= t for k in range(1, STANDARDS - 1)]

    def pick(values):
        got = jnp.full((1, PTS), values[0], jnp.int32)
        for mask, value in zip(later, values[1:]):
            got = jnp.where(mask, value, got)
        return got.astype(F32)

    lib_at = pick([lib[k] for k in range(STANDARDS - 1)])
    lib_gap = pick([lib[k + 1] - lib[k] for k in range(STANDARDS - 1)])
    for r in range(RUNS):
        base = pick([std[r, k] for k in range(STANDARDS - 1)])
        gap = pick([std[r, k + 1] - std[r, k] for k in range(STANDARDS - 1)])
        srcs[r] = base + (t.astype(F32) - lib_at) * (gap / lib_gap)

    tri[...] = (
        lax.broadcasted_iota(jnp.int32, (BLOCK, BLOCK), 0) < lax.broadcasted_iota(jnp.int32, (BLOCK, BLOCK), 1)
    ).astype(F32).astype(BF16)
    row = lax.broadcasted_iota(jnp.int32, (64, 1), 0)
    line, inner = row // 8, row % 8
    owner_xz = jnp.where(inner < SIDE, (line // 2) * 8 + inner * 2 + line % 2, -1)
    owner_zx = jnp.where(inner < SIDE, inner * 8 + (line // 2) * 2 + line % 2, -1)
    tag_sum = jnp.zeros((256, 128), F32)
    for b in range(BLOCKS):
        owner = own[b : b + 1, :]
        hit = (owner == lax.broadcasted_iota(jnp.int32, (OWNERS, BLOCK), 0)).astype(F32)
        before = jnp.dot(hit.astype(BF16), tri[...], preferred_element_type=F32)
        rank = jnp.sum(before * hit, axis=0, keepdims=True).astype(jnp.int32)
        place = owner * MOST + rank

        def fill(i, _):
            at = lax.broadcasted_iota(jnp.int32, (256, BLOCK), 0) + i * 256
            perm[b, pl.ds(pl.multiple_of(i * 256, 256), 256), :] = (at == place).astype(F32).astype(BF16)
            return 0

        lax.fori_loop(0, OWNERS * MOST // 256, fill, 0)
        tag = lg[b : b + 1, :] + 1
        low = (tag % 256).astype(F32)
        high = (tag // 256).astype(F32)
        parts = []
        for chosen in (owner_xz, owner_zx):
            mask = chosen == owner
            parts += [jnp.where(mask, low, 0.0), jnp.where(mask, high, 0.0)]
        lane = lax.broadcasted_iota(jnp.int32, (128, BLOCK), 0) - b * MOST
        at_slot = (lane == rank).astype(F32).astype(BF16)
        tag_sum = tag_sum + nt_dot(jnp.concatenate(parts, axis=0).astype(BF16), at_slot)
        qcol[b] = jnp.transpose(jnp.broadcast_to(q[b : b + 1, :], (128, BLOCK)))
    for order in range(2):
        both = tag_sum[order * 128 : order * 128 + 128]
        tags[order] = (both[:64] + 256.0 * both[64:]).reshape(LINE, 8, 128)

    pl.semaphore_wait(barrier, 13)
    for order in range(2):
        first = (xx, zz)[order]
        second = (zz, xx)[order]
        me = first * 2 + cc
        for df in range(SIDE):
            for dc in range(2):
                f2, c2 = (first + df) % SIDE, (cc + dc) % 2
                src, dst = tags.at[order, f2 * 2 + c2], rtags.at[order, me]
                if (df, dc) == (0, 0):
                    pltpu.make_async_copy(src, dst, tag_rsem.at[order]).start()
                else:
                    pltpu.make_async_remote_copy(
                        src_ref=src, dst_ref=dst, send_sem=tag_ssem.at[order], recv_sem=tag_rsem.at[order],
                        device_id=(yy, along(order, f2, second, c2)), device_id_type=MESH,
                    ).start()

    def send_profiles(j):
        order = j % 2
        first = (1 - order) * xx + order * zz
        second = (1 - order) * zz + order * xx
        me = first * 2 + cc
        slot = j % SLOTS
        load(j).wait()
        down = lax.broadcasted_iota(jnp.int32, (PTS, PTS), 0).astype(F32)
        warp = jnp.maximum(0.0, 1.0 - jnp.abs(srcs[j] - down)).astype(BF16)

        def block(b, _):
            rows = pl.ds(pl.multiple_of(b * BLOCK, BLOCK), BLOCK)
            seen = jnp.dot(xbuf[j % 2, rows, :], warp, preferred_element_type=F32)
            weight = qcol[b]
            logs = jnp.log(1.0 + seen)
            prof = jnp.concatenate([logs[:, :128] * weight, logs[:, 128:] * weight], axis=1).astype(BF16)
            for half in range(2):
                got = jnp.dot(perm[b, half * 512 : half * 512 + 512, :], prof, preferred_element_type=F32).astype(BF16)
                for i in range(16):
                    o = half * 16 + i
                    ox, oz, oc = o // 8, (o // 2) % 4, o % 2
                    of = (1 - order) * ox + order * oz
                    os = (1 - order) * oz + order * ox
                    sbuf[slot, b, of * 2 + oc, os] = got[i * MOST : (i + 1) * MOST]
            for df in (2, 1, 3, 0):
                for dc in (1, 0):
                    f2, c2 = (first + df) % SIDE, (cc + dc) % 2
                    src, dst = sbuf.at[slot, b, f2 * 2 + c2], rbuf.at[j, me, b]
                    if (df, dc) == (0, 0):
                        pltpu.make_async_copy(src, dst, r_sem.at[j]).start()
                    else:
                        pltpu.make_async_remote_copy(
                            src_ref=src, dst_ref=dst, send_sem=s_sem.at[slot], recv_sem=r_sem.at[j],
                            device_id=(yy, along(order, f2, second, c2)), device_id_type=MESH,
                        ).start()
            return 0

        lax.fori_loop(0, BLOCKS, block, 0)

    def wait_sent(slot):
        some = sbuf.at[slot, :, 0 : LINE - 1]
        pltpu.make_async_copy(some, some, s_sem.at[slot]).wait()

    def members():
        for order in range(2):
            pltpu.make_async_copy(rtags.at[order], rtags.at[order], tag_rsem.at[order]).wait()
            some = tags.at[order, 0 : LINE - 1]
            pltpu.make_async_copy(some, some, tag_ssem.at[order]).wait()

            def fill(src, _):
                got = rtags[order, src]
                group = lax.broadcasted_iota(jnp.int32, (GRP, 128), 0).astype(F32) + 1.0
                cols = pl.ds(pl.multiple_of(src * 128, 128), 128)
                for s in range(SIDE):
                    member[order, s, :, cols] = (group == got[s : s + 1]).astype(F32).astype(BF16)
                return 0

            lax.fori_loop(0, LINE, fill, 0)

    def send_sums(j):
        order = j % 2
        first = (1 - order) * xx + order * zz
        second = (1 - order) * zz + order * xx
        slot = j % SLOTS
        pltpu.make_async_copy(rbuf.at[j], rbuf.at[j], r_sem.at[j]).wait()

        def total(s):
            rows = rbuf[j, :, :, s].reshape(LINE * BLOCKS * MOST, PTS)
            return jnp.dot(member[order, s], rows, preferred_element_type=F32)

        def other(i, _):
            k = (i + 1) % 3 + 1
            s = (second + k) % SIDE
            dbuf[slot, k - 1] = total(s).astype(BF16)
            pltpu.make_async_remote_copy(
                src_ref=dbuf.at[slot, k - 1], dst_ref=ddbuf.at[j, k - 1], send_sem=d_sem.at[slot], recv_sem=dd_sem.at[j],
                device_id=(yy, along(order, first, s, cc)), device_id_type=MESH,
            ).start()
            return 0

        lax.fori_loop(0, SIDE - 1, other, 0)
        mine[slot] = total(second)

    def wait_sums(slot):
        pltpu.make_async_copy(dbuf.at[slot], dbuf.at[slot], d_sem.at[slot]).wait()

    def finish(j):
        pltpu.make_async_copy(ddbuf.at[j], ddbuf.at[j], dd_sem.at[j]).wait()
        whole = mine[j % SLOTS]
        for k in range(SIDE - 1):
            whole = whole + ddbuf[j, k].astype(F32)
        out[j] = (0.25 * whole).astype(BF16)

    def step(j, _):
        @pl.when(j < RUNS)
        def _():
            @pl.when(j >= SLOTS)
            def _():
                wait_sent(j % SLOTS)

            send_profiles(j)

            @pl.when(j + 2 < RUNS)
            def _():
                load(j + 2).start()

        @pl.when(j == 1)
        def _():
            members()

        @pl.when((j >= 2) & (j < RUNS + 2))
        def _():
            @pl.when(j - 2 >= SLOTS)
            def _():
                wait_sums((j - 2) % SLOTS)

            send_sums(j - 2)

        @pl.when(j >= 4)
        def _():
            finish(j - 4)

        return 0

    lax.fori_loop(0, RUNS + 4, step, 0)
    for slot in range(SLOTS):
        wait_sent(slot)
        wait_sums(slot)


def per_device(chromatograms, standards, library, owner_of, local_group, quality):
    vmem = pl.BlockSpec(memory_space=pltpu.VMEM)
    smem = pl.BlockSpec(memory_space=pltpu.SMEM)
    return pl.pallas_call(
        kernel,
        out_shape=jax.ShapeDtypeStruct((RUNS, GRP, PTS), BF16),
        in_specs=[pl.BlockSpec(memory_space=pl.ANY), smem, smem, vmem, vmem, vmem],
        out_specs=vmem,
        scratch_shapes=[
            pltpu.VMEM((2, BLOCKS * BLOCK, PTS), BF16),
            pltpu.VMEM((BLOCKS, OWNERS * MOST, BLOCK), BF16),
            pltpu.VMEM((BLOCK, BLOCK), BF16),
            pltpu.VMEM((BLOCKS, BLOCK, 128), F32),
            pltpu.VMEM((RUNS, 1, PTS), F32),
            pltpu.VMEM((2, LINE, 8, 128), F32),
            pltpu.VMEM((2, LINE, 8, 128), F32),
            pltpu.VMEM((2, SIDE, GRP, LINE * BLOCKS * MOST), BF16),
            pltpu.VMEM((SLOTS, BLOCKS, LINE, SIDE, MOST, PTS), BF16),
            pltpu.VMEM((RUNS, LINE, BLOCKS, SIDE, MOST, PTS), BF16),
            pltpu.VMEM((SLOTS, SIDE - 1, GRP, PTS), BF16),
            pltpu.VMEM((RUNS, SIDE - 1, GRP, PTS), BF16),
            pltpu.VMEM((SLOTS, GRP, PTS), F32),
            pltpu.SemaphoreType.DMA((2,)),
            pltpu.SemaphoreType.DMA((2,)),
            pltpu.SemaphoreType.DMA((2,)),
            pltpu.SemaphoreType.DMA((SLOTS,)),
            pltpu.SemaphoreType.DMA((RUNS,)),
            pltpu.SemaphoreType.DMA((SLOTS,)),
            pltpu.SemaphoreType.DMA((RUNS,)),
        ],
        compiler_params=pltpu.CompilerParams(
            collective_id=0, has_side_effects=True, vmem_limit_bytes=62 * 2**20
        ),
    )(
        chromatograms,
        standards,
        library,
        owner_of.reshape(BLOCKS, BLOCK),
        local_group.reshape(BLOCKS, BLOCK),
        quality.astype(F32).reshape(BLOCKS, BLOCK),
    )


def solution(mesh):
    placed = (P("run", "prec", None), P("run", None), P(), P("prec", None), P("prec"), P("prec"))
    return jax.shard_map(
        per_device, mesh=mesh, in_specs=placed, out_specs=P("run", "prec", None), check_vma=False
    )
```

time: 409 us -> 162 us (0.40)
  the two profiles are of different devices: /device:TPU:52 before, /device:TPU:1 now
where the time goes in v1:
time: 162 us
  Pallas kernels  154 us (95%)
  local copies, waits for them, and re-layouts  6.75 us (4%)
    pallas_call x1, Pallas kernels, per_device(): pl.pallas_call(kernel, out_shape=jax.ShapeDtypeStruct((RUNS, GRP, PTS), B...  154 us
    unnamed x2, local copies, waits for them, and re-layouts  3.56 us

profile of v1, /device:TPU:1, one launch (start us, length us, event | category | flops | bytes accessed | tf_op | source)
XLA Modules:
  0.0 162.0 jit_solution(4743886018574031671)
XLA Ops:
  0.0 0.5 broadcast.3
  0.5 1.4 reduce.3
  1.9 0.6 reshape.11.own
  2.5 1.3 reshape.12.lg
  3.8 1.3 reshape.16.q
  5.1 153.8 %shard_map.64 = bf16[8,512,256]{2,1,0:T(8,128)(2,1)} custom-call(bf16[8,2048,256]{2,1,0:T(8,128)(2,1)} %x_hbm.1, s32[8,11]{1,0:T(8,128)} %std.1, s32[11]{0:T(128)} %lib.1, s32[4,512]{1,0:T(4,128)} %reshape.11.own, s32[4,512]{1,0:T(4,128)} %reshape.12.lg, f32[4,512]{1,0:T(4,128)} %reshape.16.q), custom_call_target="tpu_custom_call" | custom-call | tf_op jit(solution)/shard_map/pallas_call | solution.py:260
  158.9 3.0 %copy.8 = bf16[8,512,256]{2,1,0:T(8,128)(2,1)} copy(bf16[8,512,256]{2,1,0:T(8,128)(2,1)} %shard_map.64) | data formatting | bytes 4194304

commit v2 on v1

v2 whole, which is shorter than its diff:
```python
import jax
import jax.numpy as jnp
from jax import lax
from jax.experimental import pallas as pl
from jax.experimental.pallas import tpu as pltpu
from jax.sharding import PartitionSpec as P

MESH = pl.DeviceIdType.MESH
F32 = jnp.float32
BF16 = jnp.bfloat16
RUNS = 8
BLOCKS = 4
BLOCK = 512
MOST = 32
OWNERS = 32
GRP = 512
PTS = 256
STANDARDS = 11
SIDE = 4
SLOTS = 4

LEAVES = (
    ((1, 0), ((2, 3), (3, 0), (3, 1))),
    ((0, 1), ((1, 0), (2, 0), (3, 2))),
    ((0, 3), ((0, 2), (1, 2), (2, 2))),
    ((3, 0), ((1, 3),)),
)
INNER = (((2, 1), (3, 0), 0), ((3, 3), (1, 0), 0), ((1, 1), (3, 0), 1), ((0, 3), (0, 1), 1), ((0, 1), (0, 3), 2))
ROOT = (0, 0)
NODES = tuple(n for n, _, _ in INNER) + (ROOT,)
SELF = 2 * sum(len(ps) for _, ps in LEAVES)


def layout():
    place, feeds, base = {}, {n: [n] for n in NODES}, 0
    for (sx, sz), ps in LEAVES:
        for i, (px, pz) in enumerate(ps):
            place[px, pz] = (base + i, len(ps))
            feeds[(px + sx) % SIDE, (pz + sz) % SIDE].append((px, pz))
        base += 2 * len(ps)
    for i, n in enumerate(NODES):
        place[n] = (base + i, len(NODES))
    return place, feeds


PLACE, FEEDS = layout()
CHUNKS = {n: [PLACE[p][0] + core * PLACE[p][1] for p in FEEDS[n] for core in range(2)] for n in NODES}
ORDER = [chunk for n in NODES for chunk in CHUNKS[n]]
COLUMN = {n: 128 * sum(len(CHUNKS[m]) for m in NODES[:i]) for i, n in enumerate(NODES)}


def nt_dot(a, b):
    return lax.dot_general(a, b, (((1,), (1,)), ((), ())), preferred_element_type=F32)


def to_bf16(mask):
    return mask.astype(F32).astype(BF16)


def kernel(
    x_hbm, std, lib, own, lg, q, out,
    xbuf, perm, tri, qall, qcol, srcs, tags, rtags, member, sbuf, rbuf, dbuf, ddbuf,
    x_sem, tag_ssem, tag_rsem, s_sem, r_sem, d_sem, dd_sem,
):
    yy = lax.axis_index("run")
    pp = lax.axis_index("prec")
    xx, zz, cc = pp // 8, (pp // 2) % 4, pp % 2

    def device(step, core):
        return (yy, ((xx + step[0]) % SIDE) * 8 + ((zz + step[1]) % SIDE) * 2 + core)

    def load(j):
        return pltpu.make_async_copy(x_hbm.at[j], xbuf.at[j % 2], x_sem.at[j % 2])

    barrier = pltpu.get_barrier_semaphore()
    for step, _ in LEAVES:
        for core in range(2):
            pl.semaphore_signal(barrier, inc=1, device_id=device(step, core), device_id_type=MESH)
    pl.semaphore_signal(barrier, inc=1, device_id=device(ROOT, 1 - cc), device_id_type=MESH)
    load(0).start()
    load(1).start()

    t = lax.broadcasted_iota(jnp.int32, (1, PTS), 1)
    later = [lib[k] <= t for k in range(1, STANDARDS - 1)]

    def pick(values):
        got = jnp.full((1, PTS), values[0], jnp.int32)
        for mask, value in zip(later, values[1:]):
            got = jnp.where(mask, value, got)
        return got.astype(F32)

    lib_at = pick([lib[k] for k in range(STANDARDS - 1)])
    lib_gap = pick([lib[k + 1] - lib[k] for k in range(STANDARDS - 1)])
    for r in range(RUNS):
        base = pick([std[r, k] for k in range(STANDARDS - 1)])
        gap = pick([std[r, k + 1] - std[r, k] for k in range(STANDARDS - 1)])
        srcs[r] = base + (t.astype(F32) - lib_at) * (gap / lib_gap)
    tri[...] = to_bf16(
        lax.broadcasted_iota(jnp.int32, (BLOCK, BLOCK), 0) < lax.broadcasted_iota(jnp.int32, (BLOCK, BLOCK), 1)
    )
    qall[...] = q[...].astype(F32)
    tags[...] = jnp.zeros_like(tags)

    def place_block(b):
        def lanes(ref):
            return jnp.concatenate([ref[pl.ds(b * 4 + i, 1), :] for i in range(4)], axis=1)

        owner = lanes(own)
        px = (xx + SIDE - owner // 8) % SIDE
        pz = (zz + SIDE - (owner // 2) % 4) % SIDE
        core = owner % 2
        chunk = jnp.zeros_like(owner)
        for (kx, kz), (start, apart) in PLACE.items():
            chunk = jnp.where((px == kx) & (pz == kz), start + core * apart, chunk)
        hit = (chunk == lax.broadcasted_iota(jnp.int32, (OWNERS, BLOCK), 0)).astype(F32)
        before = jnp.dot(hit.astype(BF16), tri[...], preferred_element_type=F32)
        rank = jnp.sum(before * hit, axis=0, keepdims=True).astype(jnp.int32)
        place = chunk * MOST + rank
        for i in range(4):
            at = lax.broadcasted_iota(jnp.int32, (256, BLOCK), 0) + i * 256
            perm[b, i * 256 : i * 256 + 256, :] = to_bf16(at == place)
        tag = lanes(lg) + 1
        low = hit * (tag % 256).astype(F32)
        high = hit * (tag // 256).astype(F32)
        at_slot = to_bf16(lax.broadcasted_iota(jnp.int32, (128, BLOCK), 0) - b * MOST == rank)
        both = nt_dot(jnp.concatenate([low, high], axis=0).astype(BF16), at_slot)
        tags[...] += jnp.broadcast_to((both[:OWNERS] + 256.0 * both[OWNERS:])[:, None, :], tags.shape)
        for i in range(4):
            weights = qall[pl.ds(b * 4 + i, 1), :]
            qcol[b, i * 128 : i * 128 + 128, :] = jnp.transpose(jnp.broadcast_to(weights, (128, 128)))

    def send_chunks(source, target, send_sem, recv_sem):
        base = 0
        for step, ps in LEAVES:
            n = len(ps)
            for core in range(2):
                pltpu.make_async_remote_copy(
                    src_ref=source.at[pl.ds(base + core * n, n)], dst_ref=target.at[pl.ds(base + cc * n, n)],
                    send_sem=send_sem, recv_sem=recv_sem, device_id=device(step, core), device_id_type=MESH,
                ).start()
            base += 2 * n
        n = len(NODES)
        mine, other = pl.ds(SELF + cc * n, n), pl.ds(SELF + (1 - cc) * n, n)
        pltpu.make_async_remote_copy(
            src_ref=source.at[other], dst_ref=target.at[mine],
            send_sem=send_sem, recv_sem=recv_sem, device_id=device(ROOT, 1 - cc), device_id_type=MESH,
        ).start()
        pltpu.make_async_copy(source.at[mine], target.at[mine], recv_sem).start()

    def wait_bytes(ref, sem):
        pltpu.make_async_copy(ref, ref, sem).wait()

    def send_profiles(j):
        slot = j % SLOTS
        load(j).wait()
        down = lax.broadcasted_iota(jnp.int32, (PTS, PTS), 0).astype(F32)
        warp = jnp.maximum(0.0, 1.0 - jnp.abs(srcs[j] - down)).astype(BF16)

        def block(b, _):
            @pl.when(j == 0)
            def _():
                place_block(b)

            rows = pl.ds(pl.multiple_of(b * BLOCK, BLOCK), BLOCK)
            seen = jnp.dot(xbuf[j % 2, rows, :], warp, preferred_element_type=F32)
            weight = qcol[b]
            logs = jnp.log(1.0 + seen)
            prof = jnp.concatenate([logs[:, :128] * weight, logs[:, 128:] * weight], axis=1).astype(BF16)
            for half in range(2):
                got = jnp.dot(perm[b, half * 512 : half * 512 + 512, :], prof, preferred_element_type=F32)
                sbuf[slot, b, half * 16 : half * 16 + 16] = got.astype(BF16).reshape(16, MOST, PTS)

            @pl.when((j == 0) & (b == 0))
            def _():
                pl.semaphore_wait(barrier, 9)

            send_chunks(sbuf.at[slot, b], rbuf.at[j, b], s_sem.at[slot], r_sem.at[j])
            return 0

        lax.fori_loop(0, BLOCKS, block, 0)

    def wait_sent(slot):
        wait_bytes(sbuf.at[slot, :, 0 : SELF + len(NODES)], s_sem.at[slot])

    def members():
        wait_bytes(rtags, tag_rsem)
        wait_bytes(tags.at[0 : SELF + len(NODES)], tag_ssem)
        group = lax.broadcasted_iota(jnp.int32, (GRP, 128), 0).astype(F32) + 1.0
        for i, chunk in enumerate(ORDER):
            member[:, i * 128 : i * 128 + 128] = to_bf16(group == rtags[chunk, 0:1, :])

    def total(j, node):
        rows = jnp.concatenate([rbuf[j, :, chunk].reshape(BLOCKS * MOST, PTS) for chunk in CHUNKS[node]], axis=0)
        columns = member[:, COLUMN[node] : COLUMN[node] + 128 * len(CHUNKS[node])]
        return jnp.dot(columns, rows, preferred_element_type=F32)

    def children(node):
        return [
            i for i, ((nx, nz), (sx, sz), _) in enumerate(INNER) if ((nx + sx) % SIDE, (nz + sz) % SIDE) == node
        ]

    def of_level(level):
        return [i for i, (_, _, at) in enumerate(INNER) if at == level]

    def sums_of(buffer, slot, level):
        these = of_level(level)
        return buffer.at[slot, these[0] : these[-1] + 1]

    def send_sums(j, level):
        slot = j % SLOTS
        if level == 0:
            wait_bytes(rbuf.at[j], r_sem.at[j])
        else:
            wait_bytes(sums_of(ddbuf, j, level - 1), dd_sem.at[level - 1, j])

        @pl.when(j >= SLOTS)
        def _():
            wait_bytes(sums_of(dbuf, slot, level), d_sem.at[level, slot])

        for i in of_level(level):
            node, step, _ = INNER[i]
            whole = total(j, node)
            for child in children(node):
                whole = whole + ddbuf[j, child].astype(F32)
            dbuf[slot, i] = whole.astype(BF16)
            pltpu.make_async_remote_copy(
                src_ref=dbuf.at[slot, i], dst_ref=ddbuf.at[j, i], send_sem=d_sem.at[level, slot],
                recv_sem=dd_sem.at[level, j], device_id=device(step, cc), device_id_type=MESH,
            ).start()

    def finish(j):
        wait_bytes(sums_of(ddbuf, j, 2), dd_sem.at[2, j])
        whole = total(j, ROOT)
        for child in children(ROOT):
            whole = whole + ddbuf[j, child].astype(F32)
        out[j] = (0.25 * whole).astype(BF16)

    def step(j, _):
        @pl.when(j < RUNS)
        def _():
            @pl.when(j >= SLOTS)
            def _():
                wait_sent(j % SLOTS)

            send_profiles(j)

            @pl.when(j + 2 < RUNS)
            def _():
                load(j + 2).start()

        @pl.when(j == 0)
        def _():
            send_chunks(tags, rtags, tag_ssem, tag_rsem)

        @pl.when(j == LAG - 1)
        def _():
            members()

        for level in range(3):
            @pl.when((j >= level + LAG) & (j < RUNS + level + LAG))
            def _(level=level):
                send_sums(j - level - LAG, level)

        @pl.when(j >= 3 + LAG)
        def _():
            finish(j - 3 - LAG)

        return 0

    lax.fori_loop(0, RUNS + 3 + LAG, step, 0)
    for slot in range(SLOTS):
        wait_sent(slot)
        for level in range(3):
            wait_bytes(sums_of(dbuf, slot, level), d_sem.at[level, slot])


LAG = 1


def per_device(chromatograms, standards, library, owner_of, local_group, quality):
    vmem = pl.BlockSpec(memory_space=pltpu.VMEM)
    smem = pl.BlockSpec(memory_space=pltpu.SMEM)
    chunk = (OWNERS, MOST, PTS)
    return pl.pallas_call(
        kernel,
        out_shape=jax.ShapeDtypeStruct((RUNS, GRP, PTS), BF16),
        in_specs=[pl.BlockSpec(memory_space=pl.ANY), smem, smem, vmem, vmem, vmem],
        out_specs=vmem,
        scratch_shapes=[
            pltpu.VMEM((2, BLOCKS * BLOCK, PTS), BF16),
            pltpu.VMEM((BLOCKS, OWNERS * MOST, BLOCK), BF16),
            pltpu.VMEM((BLOCK, BLOCK), BF16),
            pltpu.VMEM((16, 128), F32),
            pltpu.VMEM((BLOCKS, BLOCK, 128), F32),
            pltpu.VMEM((RUNS, 1, PTS), F32),
            pltpu.VMEM((OWNERS, 8, 128), F32),
            pltpu.VMEM((OWNERS, 8, 128), F32),
            pltpu.VMEM((GRP, OWNERS * 128), BF16),
            pltpu.VMEM((SLOTS, BLOCKS, *chunk), BF16),
            pltpu.VMEM((RUNS, BLOCKS, *chunk), BF16),
            pltpu.VMEM((SLOTS, len(INNER), GRP, PTS), BF16),
            pltpu.VMEM((RUNS, len(INNER), GRP, PTS), BF16),
            pltpu.SemaphoreType.DMA((2,)),
            pltpu.SemaphoreType.DMA,
            pltpu.SemaphoreType.DMA,
            pltpu.SemaphoreType.DMA((SLOTS,)),
            pltpu.SemaphoreType.DMA((RUNS,)),
            pltpu.SemaphoreType.DMA((3, SLOTS)),
            pltpu.SemaphoreType.DMA((3, RUNS)),
        ],
        compiler_params=pltpu.CompilerParams(collective_id=0, has_side_effects=True, vmem_limit_bytes=62 * 2**20),
    )(
        chromatograms,
        standards,
        library,
        owner_of.reshape(16, 128),
        local_group.reshape(16, 128),
        quality.reshape(16, 128),
    )


def solution(mesh):
    placed = (P("run", "prec", None), P("run", None), P(), P("prec", None), P("prec"), P("prec"))
    return jax.shard_map(
        per_device, mesh=mesh, in_specs=placed, out_specs=P("run", "prec", None), check_vma=False
    )
```

time: 162 us -> 147 us (0.907)
  Pallas kernels: 154 us -> 143 us
  local copies, waits for them, and re-layouts: 6.75 us -> 3.05 us
    pallas_call x1, Pallas kernels: 154 us -> 143 us  [per_device(): pl.pallas_call(kernel, out_shape=jax.ShapeDtypeStruct((RUNS, GRP, PTS), B...]
    reshape x3 -> x0, local copies, waits for them, and re-layouts: 3.19 us -> none  [the longest x1 1.3 us: per_device(): local_group.reshape(BLOCKS, BLOCK)]
    unnamed x2 -> x1, local copies, waits for them, and re-layouts: 3.56 us -> 3.05 us
where the time goes in v2:
time: 147 us; the launch traced here: 146 us
  Pallas kernels  143 us (97%)
  local copies, waits for them, and re-layouts  3.05 us (2%)
    pallas_call x1, Pallas kernels, per_device(): pl.pallas_call(kernel, out_shape=jax.ShapeDtypeStruct((RUNS, GRP, PTS), B...  143 us
    unnamed x1, local copies, waits for them, and re-layouts  3.05 us

profile of v2, /device:TPU:1, one launch (start us, length us, event | category | flops | bytes accessed | tf_op | source)
XLA Modules:
  0.0 146.3 jit_solution(18283886013093236131)
XLA Ops:
  0.0 143.3 %shard_map.64 = bf16[8,512,256]{2,1,0:T(8,128)(2,1)} custom-call(bf16[8,2048,256]{2,1,0:T(8,128)(2,1)} %x_hbm.1, s32[8,11]{1,0:T(8,128)} %std.1, s32[11]{0:T(128)} %lib.1, s32[16,128]{1,0:T(8,128)} %bitcast.3, s32[16,128]{1,0:T(8,128)} %bitcast.4, bf16[16,128]{1,0:T(8,128)(2,1)} %bitcast.5), custom_call_target="tpu_custom_call" | custom-call | tf_op jit(solution)/shard_map/pallas_call | solution.py:284
  143.3 3.0 %copy.8 = bf16[8,512,256]{2,1,0:T(8,128)(2,1)} copy(bf16[8,512,256]{2,1,0:T(8,128)(2,1)} %shard_map.64) | data formatting | bytes 4194304

commit v3 on v2

--- a/solution.py
+++ b/solution.py
@@ -14,10 +14,12 @@
 MOST = 32
 OWNERS = 32
 GRP = 512
+HALF = GRP // 2
 PTS = 256
 STANDARDS = 11
 SIDE = 4
 SLOTS = 4
+LAG = 3
 
 LEAVES = (
     ((1, 0), ((2, 3), (3, 0), (3, 1))),
@@ -67,7 +69,8 @@
     xx, zz, cc = pp // 8, (pp // 2) % 4, pp % 2
 
     def device(step, core):
-        return (yy, ((xx + step[0]) % SIDE) * 8 + ((zz + step[1]) % SIDE) * 2 + core)
+        sign = 1 - 2 * core
+        return (yy, ((xx + SIDE + sign * step[0]) % SIDE) * 8 + ((zz + SIDE + sign * step[1]) % SIDE) * 2 + core)
 
     def load(j):
         return pltpu.make_async_copy(x_hbm.at[j], xbuf.at[j % 2], x_sem.at[j % 2])
@@ -106,9 +109,10 @@
             return jnp.concatenate([ref[pl.ds(b * 4 + i, 1), :] for i in range(4)], axis=1)
 
         owner = lanes(own)
-        px = (xx + SIDE - owner // 8) % SIDE
-        pz = (zz + SIDE - (owner // 2) % 4) % SIDE
         core = owner % 2
+        sign = 1 - 2 * core
+        px = (SIDE + sign * (xx - owner // 8)) % SIDE
+        pz = (SIDE + sign * (zz - (owner // 2) % 4)) % SIDE
         chunk = jnp.zeros_like(owner)
         for (kx, kz), (start, apart) in PLACE.items():
             chunk = jnp.where((px == kx) & (pz == kz), start + core * apart, chunk)
@@ -189,51 +193,37 @@
         for i, chunk in enumerate(ORDER):
             member[:, i * 128 : i * 128 + 128] = to_bf16(group == rtags[chunk, 0:1, :])
 
-    def total(j, node):
+    def total(j, node, half):
         rows = jnp.concatenate([rbuf[j, :, chunk].reshape(BLOCKS * MOST, PTS) for chunk in CHUNKS[node]], axis=0)
-        columns = member[:, COLUMN[node] : COLUMN[node] + 128 * len(CHUNKS[node])]
-        return jnp.dot(columns, rows, preferred_element_type=F32)
-
-    def children(node):
-        return [
-            i for i, ((nx, nz), (sx, sz), _) in enumerate(INNER) if ((nx + sx) % SIDE, (nz + sz) % SIDE) == node
-        ]
-
-    def of_level(level):
-        return [i for i, (_, _, at) in enumerate(INNER) if at == level]
-
-    def sums_of(buffer, slot, level):
-        these = of_level(level)
-        return buffer.at[slot, these[0] : these[-1] + 1]
+        groups = member[half * HALF : half * HALF + HALF, COLUMN[node] : COLUMN[node] + 128 * len(CHUNKS[node])]
+        whole = jnp.dot(groups, rows, preferred_element_type=F32)
+        for i, ((nx, nz), (sx, sz), _) in enumerate(INNER):
+            if ((nx + sx) % SIDE, (nz + sz) % SIDE) == node:
+                wait_bytes(ddbuf.at[j, i, half], dd_sem.at[i, half, j])
+                whole = whole + ddbuf[j, i, half].astype(F32)
+        return whole
 
     def send_sums(j, level):
         slot = j % SLOTS
         if level == 0:
             wait_bytes(rbuf.at[j], r_sem.at[j])
-        else:
-            wait_bytes(sums_of(ddbuf, j, level - 1), dd_sem.at[level - 1, j])
-
-        @pl.when(j >= SLOTS)
-        def _():
-            wait_bytes(sums_of(dbuf, slot, level), d_sem.at[level, slot])
-
-        for i in of_level(level):
-            node, step, _ = INNER[i]
-            whole = total(j, node)
-            for child in children(node):
-                whole = whole + ddbuf[j, child].astype(F32)
-            dbuf[slot, i] = whole.astype(BF16)
-            pltpu.make_async_remote_copy(
-                src_ref=dbuf.at[slot, i], dst_ref=ddbuf.at[j, i], send_sem=d_sem.at[level, slot],
-                recv_sem=dd_sem.at[level, j], device_id=device(step, cc), device_id_type=MESH,
-            ).start()
+        for i, (node, step, at) in enumerate(INNER):
+            if at == level:
+
+                @pl.when(j >= SLOTS)
+                def _(i=i):
+                    wait_bytes(dbuf.at[slot, i], d_sem.at[i, slot])
+
+                for half in range(2):
+                    dbuf[slot, i, half] = total(j, node, half).astype(BF16)
+                    pltpu.make_async_remote_copy(
+                        src_ref=dbuf.at[slot, i, half], dst_ref=ddbuf.at[j, i, half], send_sem=d_sem.at[i, slot],
+                        recv_sem=dd_sem.at[i, half, j], device_id=device(step, cc), device_id_type=MESH,
+                    ).start()
 
     def finish(j):
-        wait_bytes(sums_of(ddbuf, j, 2), dd_sem.at[2, j])
-        whole = total(j, ROOT)
-        for child in children(ROOT):
-            whole = whole + ddbuf[j, child].astype(F32)
-        out[j] = (0.25 * whole).astype(BF16)
+        for half in range(2):
+            out[j, half * HALF : half * HALF + HALF] = (0.25 * total(j, ROOT, half)).astype(BF16)
 
     def step(j, _):
         @pl.when(j < RUNS)
@@ -270,11 +260,8 @@
     lax.fori_loop(0, RUNS + 3 + LAG, step, 0)
     for slot in range(SLOTS):
         wait_sent(slot)
-        for level in range(3):
-            wait_bytes(sums_of(dbuf, slot, level), d_sem.at[level, slot])
-
-
-LAG = 1
+        for i in range(len(INNER)):
+            wait_bytes(dbuf.at[slot, i], d_sem.at[i, slot])
 
 
 def per_device(chromatograms, standards, library, owner_of, local_group, quality):
@@ -298,15 +285,15 @@
             pltpu.VMEM((GRP, OWNERS * 128), BF16),
             pltpu.VMEM((SLOTS, BLOCKS, *chunk), BF16),
             pltpu.VMEM((RUNS, BLOCKS, *chunk), BF16),
-            pltpu.VMEM((SLOTS, len(INNER), GRP, PTS), BF16),
-            pltpu.VMEM((RUNS, len(INNER), GRP, PTS), BF16),
+            pltpu.VMEM((SLOTS, len(INNER), 2, HALF, PTS), BF16),
+            pltpu.VMEM((RUNS, len(INNER), 2, HALF, PTS), BF16),
             pltpu.SemaphoreType.DMA((2,)),
             pltpu.SemaphoreType.DMA,
             pltpu.SemaphoreType.DMA,
             pltpu.SemaphoreType.DMA((SLOTS,)),
             pltpu.SemaphoreType.DMA((RUNS,)),
-            pltpu.SemaphoreType.DMA((3, SLOTS)),
-            pltpu.SemaphoreType.DMA((3, RUNS)),
+            pltpu.SemaphoreType.DMA((len(INNER), SLOTS)),
+            pltpu.SemaphoreType.DMA((len(INNER), 2, RUNS)),
         ],
         compiler_params=pltpu.CompilerParams(collective_id=0, has_side_effects=True, vmem_limit_bytes=62 * 2**20),
     )(

time: 147 us -> 134 us (0.912)
  Pallas kernels: 143 us -> 131 us
    pallas_call x1, Pallas kernels: 143 us -> 131 us  [per_device(): pl.pallas_call(kernel, out_shape=jax.ShapeDtypeStruct((RUNS, GRP, PTS), B...]
where the time goes in v3:
time: 134 us
  Pallas kernels  131 us (98%)
  local copies, waits for them, and re-layouts  3.05 us (2%)
    pallas_call x1, Pallas kernels, per_device(): pl.pallas_call(kernel, out_shape=jax.ShapeDtypeStruct((RUNS, GRP, PTS), B...  131 us
    unnamed x1, local copies, waits for them, and re-layouts  3.05 us

profile of v3, /device:TPU:1, one launch (start us, length us, event | category | flops | bytes accessed | tf_op | source)
XLA Modules:
  0.0 134.3 jit_solution(13997555746812078030)
XLA Ops:
  0.0 131.2 %shard_map.64 = bf16[8,512,256]{2,1,0:T(8,128)(2,1)} custom-call(bf16[8,2048,256]{2,1,0:T(8,128)(2,1)} %x_hbm.1, s32[8,11]{1,0:T(8,128)} %std.1, s32[11]{0:T(128)} %lib.1, s32[16,128]{1,0:T(8,128)} %bitcast.3, s32[16,128]{1,0:T(8,128)} %bitcast.4, bf16[16,128]{1,0:T(8,128)(2,1)} %bitcast.5), custom_call_target="tpu_custom_call" | custom-call | tf_op jit(solution)/shard_map/pallas_call | solution.py:271
  131.2 3.0 %copy.8 = bf16[8,512,256]{2,1,0:T(8,128)(2,1)} copy(bf16[8,512,256]{2,1,0:T(8,128)(2,1)} %shard_map.64) | data formatting | bytes 4194304

commit v4 on v0

v4 whole, which is shorter than its diff:
```python
import jax
import jax.numpy as jnp
from jax import lax
from jax.experimental import pallas as pl
from jax.experimental.pallas import tpu as pltpu
from jax.sharding import PartitionSpec as P

MESH = pl.DeviceIdType.MESH
F32 = jnp.float32
BF16 = jnp.bfloat16
RUNS = 8
BLOCKS = 4
BLOCK = 512
MOST = 32
OWNERS = 32
GRP = 512
HALF = GRP // 2
PTS = 256
STANDARDS = 11
SIDE = 4
LINE = 8
OTHERS = 13


def nt_dot(a, b):
    return lax.dot_general(a, b, (((1,), (1,)), ((), ())), preferred_element_type=F32)


def to_bf16(mask):
    return mask.astype(F32).astype(BF16)


def wait_bytes(ref, sem):
    pltpu.make_async_copy(ref, ref, sem).wait()


def kernel(
    x_hbm, std, lib, own, lg, q, out,
    xbuf, tri, qcol, srcs, info, infos, pbuf, rows, slots, tagbuf, member, dbuf, relay, sums, mine, fbuf,
    x_sem, info_ssem, info_rsem, s_sem, r_sem, d_sem, relay_sem, sums_sem, f_sem, out_sem,
):
    yy = lax.axis_index("run")
    pp = lax.axis_index("prec")
    xx, zz, cc = pp // 8, (pp // 2) % 4, pp % 2
    first = (1 - cc) * xx + cc * zz
    second = (1 - cc) * zz + cc * xx
    my_run = cc * SIDE + first

    def prec(order, a, b, core):
        return ((1 - order) * a + order * b) * 8 + ((1 - order) * b + order * a) * 2 + core

    def remote(src, dst, send_sem, recv_sem, target):
        pltpu.make_async_remote_copy(
            src_ref=src, dst_ref=dst, send_sem=send_sem, recv_sem=recv_sem, device_id=(yy, target), device_id_type=MESH
        ).start()

    def turn(k):
        return jnp.where(k == 0, 2, jnp.where(k == 1, 0, jnp.where(k == 2, 1, 3)))

    def job(i):
        order, df = i % 2, turn(i // 2)
        a = (1 - order) * xx + order * zz
        b = (1 - order) * zz + order * xx
        to = (a + df) % SIDE
        return order, order * SIDE + to, prec(order, to, b, order), a * 2 + cc

    def load(i):
        return pltpu.make_async_copy(x_hbm.at[job(i)[1]], xbuf.at[i % 2], x_sem.at[i % 2])

    def is_mine(i):
        return i == 2 + cc

    barrier = pltpu.get_barrier_semaphore()
    for step in range(SIDE):
        for core in range(2):
            if step:
                for other in (prec(0, (xx + step) % SIDE, zz, core), prec(0, xx, (zz + step) % SIDE, core)):
                    pl.semaphore_signal(barrier, inc=1, device_id=(yy, other), device_id_type=MESH)
    pl.semaphore_signal(barrier, inc=1, device_id=(yy, prec(0, xx, zz, 1 - cc)), device_id_type=MESH)
    load(0).start()
    load(1).start()
    info[0] = own[...]
    info[1] = lg[...]

    t = lax.broadcasted_iota(jnp.int32, (1, PTS), 1)
    later = [lib[k] <= t for k in range(1, STANDARDS - 1)]

    def pick(values):
        got = jnp.full((1, PTS), values[0], jnp.int32)
        for mask, value in zip(later, values[1:]):
            got = jnp.where(mask, value, got)
        return got.astype(F32)

    lib_at = pick([lib[k] for k in range(STANDARDS - 1)])
    lib_gap = pick([lib[k + 1] - lib[k] for k in range(STANDARDS - 1)])
    for r in range(RUNS):
        base = pick([std[r, k] for k in range(STANDARDS - 1)])
        gap = pick([std[r, k + 1] - std[r, k] for k in range(STANDARDS - 1)])
        srcs[r] = base + (t.astype(F32) - lib_at) * (gap / lib_gap)
    tri[...] = to_bf16(
        lax.broadcasted_iota(jnp.int32, (BLOCK, BLOCK), 0) < lax.broadcasted_iota(jnp.int32, (BLOCK, BLOCK), 1)
    )
    weights = q[...].astype(F32)
    for i in range(16):
        qcol[i * 128 : i * 128 + 128, :] = jnp.transpose(jnp.broadcast_to(weights[i : i + 1, :], (128, 128)))

    def start(i, b):
        _, _, target, place = job(i)
        remote(pbuf.at[i, b], rows.at[place, b], s_sem.at[i, b], r_sem.at[place, b], target)

    def sent(i, b):
        wait_bytes(pbuf.at[i, b], s_sem.at[i, b])

    def send_run(i, _):
        _, run, target, place = job(i)
        load(i).wait()
        down = lax.broadcasted_iota(jnp.int32, (PTS, PTS), 0).astype(F32)
        warp = jnp.maximum(0.0, 1.0 - jnp.abs(srcs[run] - down)).astype(BF16)

        def block(b, _):
            at = pl.ds(pl.multiple_of(b * BLOCK, BLOCK), BLOCK)
            seen = jnp.dot(xbuf[i % 2, at, :], warp, preferred_element_type=F32)
            weight = qcol[at, :]
            logs = jnp.log(1.0 + seen)
            pbuf[i, b] = jnp.concatenate([logs[:, :128] * weight, logs[:, 128:] * weight], axis=1).astype(BF16)

            @pl.when((i == 0) & (b == 0))
            def _():
                pl.semaphore_wait(barrier, OTHERS)

            @pl.when(is_mine(i))
            def _():
                pltpu.make_async_copy(pbuf.at[i, b], rows.at[place, b], r_sem.at[place, b]).start()

            @pl.when((i < SIDE) & jnp.logical_not(is_mine(i)))
            def _():
                start(i, b)

            return 0

        lax.fori_loop(0, BLOCKS, block, 0)

        @pl.when(is_mine(i))
        def _():
            pltpu.make_async_copy(info, infos.at[place], info_rsem).start()

        @pl.when(jnp.logical_not(is_mine(i)))
        def _():
            remote(info, infos.at[place], info_ssem, info_rsem, target)

        @pl.when(i + 2 < RUNS)
        def _():
            load(i + 2).start()

        return 0

    lax.fori_loop(0, RUNS, send_run, 0)

    wait_bytes(infos, info_rsem)

    def to_slots(df, core, b):
        src = ((first + SIDE - df) % SIDE) * 2 + core

        def lanes(which):
            return jnp.concatenate([infos[src, which, pl.ds(b * 4 + i, 1), :] for i in range(4)], axis=1)

        owner = lanes(0)
        hit = (owner == lax.broadcasted_iota(jnp.int32, (OWNERS, BLOCK), 0)).astype(F32)
        before = jnp.dot(hit.astype(BF16), tri[...], preferred_element_type=F32)
        rank = jnp.sum(before * hit, axis=0, keepdims=True).astype(jnp.int32)
        tag = lanes(1) + 1
        low = hit * (tag % 256).astype(F32)
        high = hit * (tag // 256).astype(F32)
        at_slot = to_bf16(lax.broadcasted_iota(jnp.int32, (128, BLOCK), 0) - b * MOST == rank)
        both = nt_dot(jnp.concatenate([low, high], axis=0).astype(BF16), at_slot)
        tags = both[:OWNERS] + 256.0 * both[OWNERS:]

        @pl.when(b == 0)
        def _():
            tagbuf[src] = tags

        @pl.when(b > 0)
        def _():
            tagbuf[src] += tags

        place = owner * MOST + rank
        wait_bytes(rows.at[src, b], r_sem.at[src, b])
        for i in range(4):
            at = lax.broadcasted_iota(jnp.int32, (256, BLOCK), 0) + i * 256
            got = jnp.dot(to_bf16(at == place), rows[src, b], preferred_element_type=F32)
            slots[i * 8 : i * 8 + 8, src, b] = got.astype(BF16).reshape(8, MOST, PTS)

    def whole_chip(df):
        def one(n, _):
            to_slots(df, n // BLOCKS, n % BLOCKS)
            return 0

        lax.fori_loop(0, 2 * BLOCKS, one, 0)

    def send_near(b):
        for i in range(SIDE, RUNS):
            start(i, b)

    whole_chip(0)
    for i in range(2):
        for b in range(BLOCKS):
            sent(i, b)
    send_near(0)
    send_near(1)
    whole_chip(2)

    def near_block(b, _):
        @pl.when(b < 2)
        def _():
            for i in range(SIDE, RUNS):
                sent(i, b)
            send_near(b + 2)

        def one(n, _):
            to_slots(1 + 2 * (n // 2), n % 2, b)
            return 0

        lax.fori_loop(0, SIDE, one, 0)
        return 0

    lax.fori_loop(0, BLOCKS, near_block, 0)

    def total(s, t):
        o = prec(cc, t // 2, s, t % 2)
        group = lax.broadcasted_iota(jnp.int32, (GRP, 128), 0).astype(F32) + 1.0
        for src in range(LINE):
            member[:, src * 128 : src * 128 + 128] = to_bf16(group == tagbuf[src, pl.ds(o, 1), :])
        return jnp.dot(member[...], slots[o].reshape(LINE * BLOCKS * MOST, PTS), preferred_element_type=F32)

    def beside(step):
        return prec(cc, first, (second + step) % SIDE, cc)

    def far(t, _):
        whole = total((second + 2) % SIDE, t).astype(BF16)
        for half in range(2):
            dbuf[0, t, half] = whole[half * HALF : half * HALF + HALF]
            remote(dbuf.at[0, t, half], relay.at[half, t], d_sem, relay_sem.at[half, t], beside((1, 3)[half]))
        return 0

    lax.fori_loop(0, LINE, far, 0)

    def near(t, _):
        for half in range(2):
            step = (1, 3)[half]
            whole = total((second + step) % SIDE, t)
            wait_bytes(relay.at[half, t], relay_sem.at[half, t])
            passed = whole[half * HALF : half * HALF + HALF] + relay[half, t].astype(F32)
            dbuf[1 + half, t, half] = passed.astype(BF16)
            dbuf[1 + half, t, 1 - half] = whole[(1 - half) * HALF : (1 - half) * HALF + HALF].astype(BF16)
            remote(dbuf.at[1 + half, t], sums.at[half, t], d_sem, sums_sem.at[half, t], beside(step))
        return 0

    lax.fori_loop(0, LINE, near, 0)

    def keep(t, _):
        mine[t] = total(second, t)
        return 0

    lax.fori_loop(0, LINE, keep, 0)

    def finish(t, _):
        whole = mine[t].reshape(2, HALF, PTS)
        for half in range(2):
            wait_bytes(sums.at[half, t], sums_sem.at[half, t])
            whole = whole + sums[half, t].astype(F32)
        done = (0.25 * whole).astype(BF16).reshape(GRP, PTS)
        here = t == first * 2 + cc

        @pl.when(here)
        def _():
            out[my_run] = done

        @pl.when(jnp.logical_not(here))
        def _():
            fbuf[t] = done
            remote(fbuf.at[t], out.at[my_run], f_sem, out_sem, prec(cc, t // 2, second, t % 2))

        return 0

    lax.fori_loop(0, LINE, finish, 0)

    wait_bytes(out.at[0 : RUNS - 1], out_sem)
    wait_bytes(fbuf.at[0 : LINE - 1], f_sem)
    wait_bytes(dbuf, d_sem)
    wait_bytes(infos.at[0 : LINE - 1], info_ssem)

    for b in range(BLOCKS):
        sent(3 - cc, b)
    for i in range(SIDE, RUNS):
        for b in (2, 3):
            sent(i, b)


def per_device(chromatograms, standards, library, owner_of, local_group, quality):
    vmem = pl.BlockSpec(memory_space=pltpu.VMEM)
    smem = pl.BlockSpec(memory_space=pltpu.SMEM)
    return pl.pallas_call(
        kernel,
        out_shape=pltpu.VMEM((RUNS, GRP, PTS), BF16),
        in_specs=[pl.BlockSpec(memory_space=pl.ANY), smem, smem, vmem, vmem, vmem],
        out_specs=vmem,
        scratch_shapes=[
            pltpu.VMEM((2, BLOCKS * BLOCK, PTS), BF16),
            pltpu.VMEM((BLOCK, BLOCK), BF16),
            pltpu.VMEM((BLOCKS * BLOCK, 128), F32),
            pltpu.VMEM((RUNS, 1, PTS), F32),
            pltpu.VMEM((2, 16, 128), jnp.int32),
            pltpu.VMEM((LINE, 2, 16, 128), jnp.int32),
            pltpu.VMEM((RUNS, BLOCKS, BLOCK, PTS), BF16),
            pltpu.VMEM((LINE, BLOCKS, BLOCK, PTS), BF16),
            pltpu.VMEM((OWNERS, LINE, BLOCKS, MOST, PTS), BF16),
            pltpu.VMEM((LINE, OWNERS, 128), F32),
            pltpu.VMEM((GRP, LINE * 128), BF16),
            pltpu.VMEM((3, LINE, 2, HALF, PTS), BF16),
            pltpu.VMEM((2, LINE, HALF, PTS), BF16),
            pltpu.VMEM((2, LINE, 2, HALF, PTS), BF16),
            pltpu.VMEM((LINE, GRP, PTS), F32),
            pltpu.VMEM((LINE, GRP, PTS), BF16),
            pltpu.SemaphoreType.DMA((2,)),
            pltpu.SemaphoreType.DMA,
            pltpu.SemaphoreType.DMA,
            pltpu.SemaphoreType.DMA((RUNS, BLOCKS)),
            pltpu.SemaphoreType.DMA((LINE, BLOCKS)),
            pltpu.SemaphoreType.DMA,
            pltpu.SemaphoreType.DMA((2, LINE)),
            pltpu.SemaphoreType.DMA((2, LINE)),
            pltpu.SemaphoreType.DMA,
            pltpu.SemaphoreType.DMA,
        ],
        compiler_params=pltpu.CompilerParams(collective_id=0, has_side_effects=True, vmem_limit_bytes=58 * 2**20),
    )(
        chromatograms,
        standards,
        library,
        owner_of.reshape(16, 128),
        local_group.reshape(16, 128),
        quality.reshape(16, 128),
    )


def solution(mesh):
    placed = (P("run", "prec", None), P("run", None), P(), P("prec", None), P("prec"), P("prec"))
    return jax.shard_map(
        per_device, mesh=mesh, in_specs=placed, out_specs=P("run", "prec", None), check_vma=False
    )
```

time: 409 us -> 129 us (0.32)
  the two profiles are of different devices: /device:TPU:52 before, /device:TPU:1 now
where the time goes in v4:
time: 129 us; the launch traced here: 127 us
  Pallas kernels  125 us (97%)
  local copies, waits for them, and re-layouts  1.32 us (1%)
    pallas_call x1, Pallas kernels, per_device(): pl.pallas_call(kernel, out_shape=pltpu.VMEM((RUNS, GRP, PTS), BF16), in_s...  125 us

profile of v4, /device:TPU:1, one launch (start us, length us, event | category | flops | bytes accessed | tf_op | source)
XLA Modules:
  0.0 126.7 jit_solution(5029874760758576199)
XLA Ops:
  0.0 125.4 %shard_map.64 = bf16[8,512,256]{2,1,0:T(8,128)(2,1)S(1)} custom-call(bf16[8,2048,256]{2,1,0:T(8,128)(2,1)} %x_hbm.1, s32[8,11]{1,0:T(8,128)} %std.1, s32[11]{0:T(128)} %lib.1, s32[16,128]{1,0:T(8,128)} %bitcast.3, s32[16,128]{1,0:T(8,128)} %bitcast.4, bf16[16,128]{1,0:T(8,128)(2,1)} %bitcast.5), custom_call_target="tpu_custom_call" | custom-call | tf_op jit(solution)/shard_map/pallas_call | solution.py:302
  125.4 1.3 %copy.8 = bf16[8,512,256]{2,1,0:T(8,128)(2,1)} copy(bf16[8,512,256]{2,1,0:T(8,128)(2,1)S(1)} %shard_map.64) | data formatting | bytes 4194304

commit v5 on v4

--- a/solution.py
+++ b/solution.py
@@ -235,7 +235,11 @@
     def beside(step):
         return prec(cc, first, (second + step) % SIDE, cc)
 
-    def far(t, _):
+    def served(n):
+        return ((first + turn(n // 2)) % SIDE) * 2 + n % 2
+
+    def far(n, _):
+        t = served(n)
         whole = total((second + 2) % SIDE, t).astype(BF16)
         for half in range(2):
             dbuf[0, t, half] = whole[half * HALF : half * HALF + HALF]
@@ -244,7 +248,8 @@
 
     lax.fori_loop(0, LINE, far, 0)
 
-    def near(t, _):
+    def near(n, _):
+        t = served(n)
         for half in range(2):
             step = (1, 3)[half]
             whole = total((second + step) % SIDE, t)
@@ -263,7 +268,8 @@
 
     lax.fori_loop(0, LINE, keep, 0)
 
-    def finish(t, _):
+    def finish(n, _):
+        t = served(n)
         whole = mine[t].reshape(2, HALF, PTS)
         for half in range(2):
             wait_bytes(sums.at[half, t], sums_sem.at[half, t])

time: 129 us -> 124 us (0.961); the launches traced: 127 us -> 124 us
  Pallas kernels: 125 us -> 122 us
    pallas_call x1, Pallas kernels: 125 us -> 122 us  [per_device(): pl.pallas_call(kernel, out_shape=pltpu.VMEM((RUNS, GRP, PTS), BF16), in_s...]
where the time goes in v5:
time: 124 us
  Pallas kernels  122 us (98%)
  local copies, waits for them, and re-layouts  1.32 us (1%)
    pallas_call x1, Pallas kernels, per_device(): pl.pallas_call(kernel, out_shape=pltpu.VMEM((RUNS, GRP, PTS), BF16), in_s...  122 us

profile of v5, /device:TPU:1, one launch (start us, length us, event | category | flops | bytes accessed | tf_op | source)
XLA Modules:
  0.0 123.5 jit_solution(11146883053327492679)
XLA Ops:
  0.0 122.2 %shard_map.64 = bf16[8,512,256]{2,1,0:T(8,128)(2,1)S(1)} custom-call(bf16[8,2048,256]{2,1,0:T(8,128)(2,1)} %x_hbm.1, s32[8,11]{1,0:T(8,128)} %std.1, s32[11]{0:T(128)} %lib.1, s32[16,128]{1,0:T(8,128)} %bitcast.3, s32[16,128]{1,0:T(8,128)} %bitcast.4, bf16[16,128]{1,0:T(8,128)(2,1)} %bitcast.5), custom_call_target="tpu_custom_call" | custom-call | tf_op jit(solution)/shard_map/pallas_call | solution.py:308
  122.2 1.3 %copy.8 = bf16[8,512,256]{2,1,0:T(8,128)(2,1)} copy(bf16[8,512,256]{2,1,0:T(8,128)(2,1)S(1)} %shard_map.64) | data formatting | bytes 4194304

commit v6 on v5

--- a/solution.py
+++ b/solution.py
@@ -20,6 +20,7 @@
 SIDE = 4
 LINE = 8
 OTHERS = 13
+BEHIND = 3
 
 
 def nt_dot(a, b):
@@ -37,7 +38,7 @@
 def kernel(
     x_hbm, std, lib, own, lg, q, out,
     xbuf, tri, qcol, srcs, info, infos, pbuf, rows, slots, tagbuf, member, dbuf, relay, sums, mine, fbuf,
-    x_sem, info_ssem, info_rsem, s_sem, r_sem, d_sem, relay_sem, sums_sem, f_sem, out_sem,
+    x_sem, info_ssem, info_rsem, s_sem, r_sem, d_sem, near_sem, relay_sem, sums_sem, f_sem, out_sem,
 ):
     yy = lax.axis_index("run")
     pp = lax.axis_index("prec")
@@ -248,28 +249,7 @@
 
     lax.fori_loop(0, LINE, far, 0)
 
-    def near(n, _):
-        t = served(n)
-        for half in range(2):
-            step = (1, 3)[half]
-            whole = total((second + step) % SIDE, t)
-            wait_bytes(relay.at[half, t], relay_sem.at[half, t])
-            passed = whole[half * HALF : half * HALF + HALF] + relay[half, t].astype(F32)
-            dbuf[1 + half, t, half] = passed.astype(BF16)
-            dbuf[1 + half, t, 1 - half] = whole[(1 - half) * HALF : (1 - half) * HALF + HALF].astype(BF16)
-            remote(dbuf.at[1 + half, t], sums.at[half, t], d_sem, sums_sem.at[half, t], beside(step))
-        return 0
-
-    lax.fori_loop(0, LINE, near, 0)
-
-    def keep(t, _):
-        mine[t] = total(second, t)
-        return 0
-
-    lax.fori_loop(0, LINE, keep, 0)
-
-    def finish(n, _):
-        t = served(n)
+    def finish(t):
         whole = mine[t].reshape(2, HALF, PTS)
         for half in range(2):
             wait_bytes(sums.at[half, t], sums_sem.at[half, t])
@@ -286,13 +266,45 @@
             fbuf[t] = done
             remote(fbuf.at[t], out.at[my_run], f_sem, out_sem, prec(cc, t // 2, second, t % 2))
 
-        return 0
-
-    lax.fori_loop(0, LINE, finish, 0)
+    def left(t):
+        wait_bytes(dbuf.at[1:3, t], near_sem.at[t])
+
+    def near(n, _):
+        t = served(n)
+        for half in range(2):
+            whole = total((second + (1, 3)[half]) % SIDE, t)
+            wait_bytes(relay.at[half, t], relay_sem.at[half, t])
+            passed = whole[half * HALF : half * HALF + HALF] + relay[half, t].astype(F32)
+            dbuf[1 + half, t, half] = passed.astype(BF16)
+            dbuf[1 + half, t, 1 - half] = whole[(1 - half) * HALF : (1 - half) * HALF + HALF].astype(BF16)
+
+        @pl.when(n >= 2)
+        def _():
+            left(served(n - 2))
+
+        for half in range(2):
+            remote(dbuf.at[1 + half, t], sums.at[half, t], near_sem.at[t], sums_sem.at[half, t], beside((1, 3)[half]))
+        mine[t] = total(second, t)
+
+        @pl.when(n >= BEHIND)
+        def _():
+            finish(served(n - BEHIND))
+
+        return 0
+
+    lax.fori_loop(0, LINE, near, 0)
+
+    def last(n, _):
+        finish(served(n))
+        return 0
+
+    lax.fori_loop(LINE - BEHIND, LINE, last, 0)
+    left(served(LINE - 2))
+    left(served(LINE - 1))
 
     wait_bytes(out.at[0 : RUNS - 1], out_sem)
     wait_bytes(fbuf.at[0 : LINE - 1], f_sem)
-    wait_bytes(dbuf, d_sem)
+    wait_bytes(dbuf.at[0], d_sem)
     wait_bytes(infos.at[0 : LINE - 1], info_ssem)
 
     for b in range(BLOCKS):
@@ -333,6 +345,7 @@
             pltpu.SemaphoreType.DMA((RUNS, BLOCKS)),
             pltpu.SemaphoreType.DMA((LINE, BLOCKS)),
             pltpu.SemaphoreType.DMA,
+            pltpu.SemaphoreType.DMA((LINE,)),
             pltpu.SemaphoreType.DMA((2, LINE)),
             pltpu.SemaphoreType.DMA((2, LINE)),
             pltpu.SemaphoreType.DMA,

time: 124 us -> 124 us (level)
  no operation moved by 1% of the time
where the time goes in v6:
time: 124 us; the launch traced here: 123 us
  Pallas kernels  122 us (98%)
  local copies, waits for them, and re-layouts  1.32 us (1%)
    pallas_call x1, Pallas kernels, per_device(): pl.pallas_call(kernel, out_shape=pltpu.VMEM((RUNS, GRP, PTS), BF16), in_s...  122 us

profile of v6, /device:TPU:1, one launch (start us, length us, event | category | flops | bytes accessed | tf_op | source)
XLA Modules:
  0.0 123.3 jit_solution(10066328182170875231)
XLA Ops:
  0.0 122.0 %shard_map.64 = bf16[8,512,256]{2,1,0:T(8,128)(2,1)S(1)} custom-call(bf16[8,2048,256]{2,1,0:T(8,128)(2,1)} %x_hbm.1, s32[8,11]{1,0:T(8,128)} %std.1, s32[11]{0:T(128)} %lib.1, s32[16,128]{1,0:T(8,128)} %bitcast.3, s32[16,128]{1,0:T(8,128)} %bitcast.4, bf16[16,128]{1,0:T(8,128)(2,1)} %bitcast.5), custom_call_target="tpu_custom_call" | custom-call | tf_op jit(solution)/shard_map/pallas_call | solution.py:320
  122.0 1.3 %copy.8 = bf16[8,512,256]{2,1,0:T(8,128)(2,1)} copy(bf16[8,512,256]{2,1,0:T(8,128)(2,1)S(1)} %shard_map.64) | data formatting | bytes 4194304
